TPU v7x, 128 devices: a whole 4x4x4 slice. The times are simulated.
128 devices in a mesh: east: 4 (over y), north: 16 (over x, z), layer: 2 (over core).
Axes of the slice: x: 4, y: 4, z: 4, core: 2. Of those that a mesh axis runs over, the one named last changes fastest.
Arguments:
- head_old: float32 [8, 2048, 1024], P('layer', 'north', 'east'), may hold values from -6 to 6
- head_target: float32 [8, 2048, 1024], P('layer', 'north', 'east'), may hold values from -12 to 12
- conductivity_east: bfloat16 [8, 2048, 1024], P('layer', 'north', 'east'), may hold values from 0.05 to 6, as said below
- conductivity_north: bfloat16 [8, 2048, 1024], P('layer', 'north', 'east'), may hold values from 0.099609375 to 2
- conductivity_vertical: bfloat16 [8, 2048, 1024], P('layer', 'north', 'east'), may hold values from 0.019897461 to 0.5
- storage: bfloat16 [8, 2048, 1024], P('layer', 'north', 'east'), may hold values from 0.19921875 to 2
- well_east: int32 [3000], replicated, may hold values from 0 to 1023
- well_north: int32 [3000], replicated, may hold values from 0 to 2047
- screen_top: int32 [3000], replicated, may hold values from 0 to 3
- screen_bottom: int32 [3000], replicated, may hold values from 3 to 7
- tariff_band: int32 [3000], replicated, may hold values from 0 to 3
- pump_rates: float32 [3000], replicated, may hold values from 0.2 to 2
- ground_level: float32 [3000], replicated, may hold values from 2 to 6
- band_prices: float32 [4], replicated, may hold values from 0.5 to 4
Outputs:
- head_new: float32 [8, 2048, 1024], P('layer', 'north', 'east')
- adjoint_head: float32 [8, 2048, 1024], P('layer', 'north', 'east')
- rate_gradient: float32 [3000], replicated
- pumping_cost: float32 [], replicated
- misfit: float32 [], replicated
Inputs may be any that keep to these rules, and one draw needn't show every extreme that they name: Every screen spans at least one layer: screen_top <= screen_bottom for each well. `conductivity_east`: conductivity along x, positive.
All inputs are finite; a program needn't handle non-finite values.
Results may differ from a plain program's by a relative error of at most 0.0003.
Values may be sent and summed in bfloat16 or wider, within the bound.
A program may use at most 128 MiB of HBM per device.

v0:
```python
import jax
import jax.numpy as jnp
from jax import lax
from jax.sharding import PartitionSpec as P

SWEEPS = 3
CENTRE = 1.0
HALF_WIDTH = 0.95


def extended(value, sides, width):
    for axis, dim in sides:
        size, length = (lax.axis_size(axis), value.shape[dim])
        up = [(i, (i + 1) % size) for i in range(size - 1)]
        down = [(j, i) for i, j in up]
        last = lax.slice_in_dim(value, length - width, length, axis=dim)
        initial = lax.slice_in_dim(value, 0, width, axis=dim)
        before = lax.ppermute(last, axis, up)
        after = lax.ppermute(initial, axis, down)
        value = jnp.concatenate([before, value, after], axis=dim)
    return value


def harmonic(first, second):
    total = first + second
    return 2.0 * first * second / jnp.where(total > 0, total, 1.0)


def face_terms(east_pad, north_pad, up_pad, stored):
    face_east = harmonic(east_pad[:, :, :-1], east_pad[:, :, 1:])
    face_north = harmonic(north_pad[:, :-1], north_pad[:, 1:])
    face_up = harmonic(up_pad[:-1], up_pad[1:])
    diagonal = stored + face_east[:, :, :-1] + face_east[:, :, 1:]
    diagonal = diagonal + face_north[:, :-1] + face_north[:, 1:]
    diagonal = diagonal + face_up[:-1] + face_up[1:]
    positive = diagonal > 0
    inverse = jnp.where(positive, 1.0 / jnp.where(positive, diagonal, 1.0), 0.0)
    return (stored, face_east, face_north, face_up, inverse)


def coefficients(padded_coefs):
    stacked = padded_coefs.astype(jnp.float32)
    east_pad = stacked[0][1:-1, 1:-1, :]
    north_pad = stacked[1][1:-1, :, 1:-1]
    up_pad = stacked[2][:, 1:-1, 1:-1]
    stored = stacked[3][1:-1, 1:-1, 1:-1]
    return face_terms(east_pad, north_pad, up_pad, stored)


def apply_operator(padded, storage_part, face_east, face_north, face_up):
    center = padded[1:-1, 1:-1, 1:-1]
    step_east = padded[1:-1, 1:-1, 1:] - padded[1:-1, 1:-1, :-1]
    step_north = padded[1:-1, 1:, 1:-1] - padded[1:-1, :-1, 1:-1]
    step_up = padded[1:, 1:-1, 1:-1] - padded[:-1, 1:-1, 1:-1]
    flux_east = face_east * step_east
    flux_north = face_north * step_north
    flux_up = face_up * step_up
    total = storage_part * center + (flux_east[:, :, :-1] - flux_east[:, :, 1:])
    total = total + (flux_north[:, :-1] - flux_north[:, 1:])
    return total + (flux_up[:-1] - flux_up[1:])


def keep_whole(field):
    return field


def chebyshev(start, rhs, operate, trim, precondition):
    if start is None:
        residual = rhs
    else:
        residual = trim(rhs) - operate(start)
    direction = precondition(residual) / CENTRE
    if start is None:
        iterate = direction
    else:
        iterate = trim(start) + direction
    sigma = CENTRE / HALF_WIDTH
    factor = 1.0 / sigma
    for sweep_index in range(SWEEPS - 1):
        residual = trim(residual) - operate(direction)
        factor_next = 1.0 / (2.0 * sigma - factor)
        direction = factor_next * factor * trim(
            direction
        ) + 2.0 * factor_next / HALF_WIDTH * precondition(residual)
        iterate = trim(iterate) + direction
        factor = factor_next
    return iterate


def per_device(
    head_old,
    head_target,
    conductivity_east,
    conductivity_north,
    conductivity_vertical,
    storage,
    well_east,
    well_north,
    screen_top,
    screen_bottom,
    tariff_band,
    pump_rates,
    ground_level,
    band_prices,
):
    depth_cells, north_cells, east_cells = head_old.shape
    stacked_coefs = jnp.stack(
        (conductivity_east, conductivity_north, conductivity_vertical, storage)
    )
    padded_coefs = extended(stacked_coefs, (("east", 3), ("north", 2), ("layer", 1)), 1)
    margin = 0
    top_level = coefficients(padded_coefs)
    levels = [None] * (margin + 1)
    levels[margin] = top_level

    def margin_of(field):
        return (field.shape[0] - depth_cells) // 2

    def precondition(residual):
        return levels[margin_of(residual)][4] * residual

    def operate(field):
        padded = extended(field, (("east", 2), ("north", 1), ("layer", 0)), 1)
        level = levels[0]
        return apply_operator(padded, level[0], level[1], level[2], level[3])

    east_start = lax.axis_index("east") * east_cells
    north_start = lax.axis_index("north") * north_cells
    layer_start = lax.axis_index("layer") * depth_cells
    local_east = well_east - east_start
    local_north = well_north - north_start
    owning = (
        (local_east >= 0)
        & (local_east < east_cells)
        & (local_north >= 0)
        & (local_north < north_cells)
    ).astype(jnp.float32)
    cells = jnp.clip(local_north, 0, north_cells - 1) * east_cells + jnp.clip(
        local_east, 0, east_cells - 1
    )
    depth = layer_start + jnp.arange(depth_cells, dtype=jnp.int32)[:, None]
    screened = ((depth >= screen_top[None, :]) & (depth <= screen_bottom[None, :])).astype(
        jnp.float32
    ) * owning[None, :]
    weights = (
        conductivity_east.reshape(depth_cells, north_cells * east_cells)[:, cells].astype(
            jnp.float32
        )
        * screened
    )
    totals = lax.psum(jnp.sum(weights, axis=0), "layer")
    shares = weights / (totals + (1.0 - owning))[None, :]
    flat_shape = (depth_cells, north_cells * east_cells)
    source = (
        jnp.zeros(flat_shape, jnp.float32)
        .at[:, cells]
        .add(pump_rates[None, :] * shares)
        .reshape(head_old.shape)
    )
    stored = storage.astype(jnp.float32)
    rhs = stored * head_old - source
    head_new = chebyshev(head_old, rhs, operate, keep_whole, precondition)
    departure = head_new - head_target
    misfit_part = jnp.sum(departure * departure)
    all_cells = float(
        depth_cells
        * north_cells
        * east_cells
        * lax.axis_size("east")
        * lax.axis_size("north")
        * lax.axis_size("layer")
    )
    head_part = jnp.sum(shares * head_new.reshape(flat_shape)[:, cells], axis=0)
    head_screen, misfit_total = lax.psum((head_part, misfit_part), ("east", "north", "layer"))
    band_ids = jnp.arange(band_prices.shape[0], dtype=jnp.int32)
    prices = jnp.sum(
        jnp.where(tariff_band[:, None] == band_ids[None, :], band_prices[None, :], 0.0), axis=1
    )
    load = (
        departure.reshape(flat_shape)
        .at[:, cells]
        .add(-(prices * pump_rates)[None, :] * shares)
        .reshape(head_old.shape)
    )
    adjoint_head = chebyshev(None, load, operate, keep_whole, precondition)
    adjoint_part = jnp.sum(shares * adjoint_head.reshape(flat_shape)[:, cells], axis=0)
    adjoint_screen = lax.psum(adjoint_part, ("east", "north", "layer"))
    misfit = misfit_total / all_cells
    lift = ground_level - head_screen
    rate_gradient = prices * lift - adjoint_screen
    pumping_cost = jnp.sum(prices * pump_rates * lift)
    return (head_new, adjoint_head, rate_gradient, pumping_cost, misfit)


def solution(mesh):
    in_specs = (
        P("layer", "north", "east"),
        P("layer", "north", "east"),
        P("layer", "north", "east"),
        P("layer", "north", "east"),
        P("layer", "north", "east"),
        P("layer", "north", "east"),
        P(),
        P(),
        P(),
        P(),
        P(),
        P(),
        P(),
        P(),
    )
    out_specs = (P("layer", "north", "east"), P("layer", "north", "east"), P(), P(), P())
    return jax.shard_map(
        per_device, mesh=mesh, in_specs=in_specs, out_specs=out_specs, check_vma=False
    )
```

profile of v0, /device:TPU:1, one launch (start us, length us, event | category | flops | bytes accessed | tf_op | source)
XLA Modules:
  0.0 416.1 jit_solution(4808711370803003127)
XLA Ops:
  0.6 1.9 fusion.86
  2.5 4.0 collective-permute-start.7
  6.6 1.3 collective-permute-start.6
  7.9 1.4 pad_maximum_fusion.1
  10.5 4.0 collective-permute-start
  14.5 1.3 collective-permute-start.1
  15.9 6.1 %copy.26 = bf16[4,128,256]{0,2,1:T(8,128)(2,1)} copy(bf16[4,128,256]{2,1,0:T(8,128)(2,1)S(1)} %copy-done.7) | data formatting | bytes 524288 | tf_op args[2]
  22.1 13.0 %gather_fusion = bf16[3000,4]{1,0:T(8,128)(2,1)S(1)} fusion(bf16[4,32768]{0,1:T(8,128)(2,1)} %bitcast.53, s32[3072]{0:T(1024)S(1)} %pad_clamp_fusion), kind=kCustom, calls=%fused_computation | custom fusion | bytes 60000 | tf_op jit(solution)/shard_map/gather | solution.py:146
  35.2 2.6 fusion.10
  37.8 4.6 %psum.28 = f32[3000]{0:T(1024)S(1)} all-reduce(f32[3000]{0:T(1024)S(1)} %fusion.10), channel_id=1, replica_groups=mesh['east'=4,'north'=16,'layer'=2] {'layer'}, use_global_device_ids=true, to_apply=%region_1.2 | all-reduce | flops 3000 | bytes 24000 | tf_op jit(solution)/shard_map/psum | solution.py:151
  43.4 3.5 collective-permute-start.2
  47.0 1.3 collective-permute-start.3
  48.4 4.2 %collective-permute-start.9 = (f32[4,1,258]{2,1,0:T(1,128)S(1)}, f32[4,1,258]{2,1,0:T(1,128)S(1)}, u32[]{:S(2)}, u32[]{:S(2)}) collective-permute-start(f32[4,1,258]{2,1,0:T(1,128)S(1)} %get-tuple-element.54), channel_id=1, source_target_pairs={{0,2},{2,4},{4,6},{6,8},{8,10},{10,12},{12,14},{14,16},{16,18},{18... | collective-permute-start | bytes 12392 | tf_op jit(solution)/shard_map/ppermute | solution.py:18
  52.6 1.3 collective-permute-start.8
  53.9 3.4 pad_maximum_fusion
  59.6 4.6 %collective-permute-start.5 = (bf16[4,1,130,258]{3,2,1,0:T(8,128)(2,1)}, bf16[4,1,130,258]{3,2,1,0:T(8,128)(2,1)}, u32[]{:S(2)}, u32[]{:S(2)}) collective-permute-start(bf16[4,1,130,258]{3,2,1,0:T(8,128)(2,1)} %get-tuple-element.33), channel_id=1, source_target_pairs={{1,0},{3,2},{5,4},{7,6},{9,8},{11,10},{13,12},{15,14},{17,16},{19,... | collective-permute-start | bytes 804968 | tf_op jit(solution)/shard_map/ppermute | solution.py:19
  64.1 26.2 %scatter_custom_fusion = f32[4,32768]{0,1:T(8,128)} fusion(s32[3000]{0:T(1024)S(1)} %compare_select_fusion.5, f32[]{:T(128)} %constant.20.clone.1, f32[3000]{0:T(1024)S(1)} %copy-done.20, bf16[3000,4]{1,0:T(8,128)(2,1)S(1)} %gather_fusion, f32[3000]{0:T(1024)S(1)} %subtract_add_fusion, f32[3000]{0:T(1024)S(1)} %and_convert_fusion, s32[4]{0:T(128)S(1)} %iota_add_fusion, ...), kind=kCustom, calls=%fused_computation.5 | custom fusion | flops 108000 | bytes 1354244 | tf_op jit(solution)/shard_map/scatter-add | solution.py:157
  90.4 10.7 %copy.27 = f32[4,128,256]{2,1,0:T(8,128)} copy(f32[4,128,256]{0,2,1:T(8,128)} %bitcast.50) | data formatting | bytes 1048576 | tf_op jit(solution)/shard_map/reshape | solution.py:158
  101.3 1.3 collective-permute-start.10
  102.6 1.5 collective-permute-start.11
  104.1 5.4 %maximum_convert_fusion = f32[4,6,130,258]{3,2,1,0:T(8,128)S(1)} fusion(bf16[4,1,130,258]{3,2,1,0:T(8,128)(2,1)} %collective-permute-done.5, bf16[4,4,1,258]{3,2,1,0:T(2,128)(2,1)S(1)} %collective-permute-done.3, bf16[4,4,128,1]{3,2,1,0:T(8,128)(2,1)} %collective-permute-done.1, bf16[1,4,128,256]{3,2,1,0:T(8,128)(2,1)S(1)} %bitcast.61, ...), kind=kLoop, calls=%fused_computation.7 | loop fusion | flops 16099200 | bytes 4829760 | tf_op jit(solution)/shard_map/convert_element_type | solution.py:42
  113.0 4.1 collective-permute-start.13
  117.1 1.3 collective-permute-start.12
  118.5 3.0 collective-permute-done.13
  121.5 3.8 collective-permute-done.12
  125.5 4.0 collective-permute-start.15
  129.5 1.3 collective-permute-start.14
  131.1 2.9 collective-permute-done.14
  134.2 5.5 %collective-permute-start.16 = (f32[1,130,258]{2,1,0:T(8,128)S(1)}, f32[1,130,258]{2,1,0:T(8,128)S(1)}, u32[]{:S(2)}, u32[]{:S(2)}) collective-permute-start(f32[1,130,258]{2,1,0:T(8,128)S(1)} %get-tuple-element.40), channel_id=1, source_target_pairs={{1,0},{3,2},{5,4},{7,6},{9,8},{11,10},{13,12},{15,14},{17,16},{19,... | collective-permute-start | bytes 402488 | tf_op jit(solution)/shard_map/ppermute | solution.py:19
  141.3 1.8 collective-permute-done.17
  144.1 3.6 collective-permute-start.19
  149.0 4.2 %collective-permute-done.19 = f32[4,128,1]{2,1,0:T(8,128)S(1)} collective-permute-done((f32[4,128,1]{2,1,0:T(8,128)S(1)}, f32[4,128,1]{2,1,0:T(8,128)S(1)}, u32[]{:S(2)}, u32[]{:S(2)}) %collective-permute-start.19) | collective-permute-done | bytes 2080 | tf_op jit(solution)/shard_map/ppermute | solution.py:18
  153.2 3.8 collective-permute-done.18
  157.1 3.6 collective-permute-start.21
  160.6 1.3 collective-permute-start.20
  162.3 4.9 %collective-permute-done.20 = f32[4,1,258]{2,1,0:T(1,128)S(1)} collective-permute-done((f32[4,1,258]{2,1,0:T(1,128)S(1)}, f32[4,1,258]{2,1,0:T(1,128)S(1)}, u32[]{:S(2)}, u32[]{:S(2)}) %collective-permute-start.20) | collective-permute-done | bytes 4160 | tf_op jit(solution)/shard_map/ppermute | solution.py:19
  167.4 4.3 %collective-permute-start.22 = (f32[1,130,258]{2,1,0:T(8,128)S(1)}, f32[1,130,258]{2,1,0:T(8,128)S(1)}, u32[]{:S(2)}, u32[]{:S(2)}) collective-permute-start(f32[1,130,258]{2,1,0:T(8,128)S(1)} %get-tuple-element.38), channel_id=1, source_target_pairs={{1,0},{3,2},{5,4},{7,6},{9,8},{11,10},{13,12},{15,14},{17,16},{19,... | collective-permute-start | bytes 402488 | tf_op jit(solution)/shard_map/ppermute | solution.py:19
  171.7 1.5 collective-permute-start.23
  173.5 1.6 collective-permute-done.23
  175.4 2.2 multiply_reduce_fusion
  177.6 9.9 %copy.28 = f32[4,128,256]{0,2,1:T(8,128)} copy(f32[4,128,256]{2,1,0:T(8,128)} %get-tuple-element.11) | data formatting | bytes 1048576 | tf_op jit(solution)/shard_map/sub | solution.py:163
  187.4 31.2 %scatter_custom_fusion.1 = f32[4,32768]{0,1:T(8,128)} fusion(f32[4,32768]{0,1:T(8,128)} %bitcast.48, s32[3000]{0:T(1024)S(1)} %compare_select_fusion.5, f32[3000]{0:T(1024)S(1)} %multiply_negate_fusion, bf16[3000,4]{1,0:T(8,128)(2,1)} %copy-done.4, f32[3000]{0:T(1024)S(1)} %subtract_add_fusion, f32[3000]{0:T(1024)S(1)} %and_convert_fusion, ...), kind=kCustom, calls=%fused_computation.16 | custom fusion | flops 108000 | bytes 1354240 | tf_op jit(solution)/shard_map/scatter-add | solution.py:182
  218.7 10.7 %copy.29 = f32[4,128,256]{2,1,0:T(8,128)} copy(f32[4,128,256]{0,2,1:T(8,128)} %bitcast.49) | data formatting | bytes 1048576 | tf_op jit(solution)/shard_map/reshape | solution.py:183
  230.6 3.2 collective-permute-start.25
  235.1 4.1 collective-permute-done.25
  239.2 3.8 collective-permute-done.24
  243.1 5.7 %collective-permute-start.27 = (f32[4,1,258]{2,1,0:T(1,128)S(1)}, f32[4,1,258]{2,1,0:T(1,128)S(1)}, u32[]{:S(2)}, u32[]{:S(2)}) collective-permute-start(f32[4,1,258]{2,1,0:T(1,128)S(1)} %get-tuple-element.46), channel_id=1, source_target_pairs={{0,2},{2,4},{4,6},{6,8},{8,10},{10,12},{12,14},{14,16},{16,18},{18... | collective-permute-start | bytes 12392 | tf_op jit(solution)/shard_map/ppermute | solution.py:18
  250.5 3.0 collective-permute-done.26
  253.8 4.5 %collective-permute-start.28 = (f32[1,130,258]{2,1,0:T(8,128)S(1)}, f32[1,130,258]{2,1,0:T(8,128)S(1)}, u32[]{:S(2)}, u32[]{:S(2)}) collective-permute-start(f32[1,130,258]{2,1,0:T(8,128)S(1)} %get-tuple-element.36), channel_id=1, source_target_pairs={{1,0},{3,2},{5,4},{7,6},{9,8},{11,10},{13,12},{15,14},{17,16},{19,... | collective-permute-start | bytes 402488 | tf_op jit(solution)/shard_map/ppermute | solution.py:19
  258.2 1.3 collective-permute-start.29
  259.8 1.8 collective-permute-done.29
  261.9 2.5 multiply_add_fusion
  265.3 1.9 collective-permute-start.31
  268.5 9.7 %copy.31 = f32[4,128,256]{0,2,1:T(8,128)} copy(f32[4,128,256]{2,1,0:T(8,128)} %get-tuple-element.12) | data formatting | bytes 1048576 | tf_op jit(solution)/shard_map/add | solution.py:85
  278.1 16.6 %gather_fusion.1 = f32[3000,4]{1,0:T(8,128)} fusion(f32[4,32768]{0,1:T(8,128)} %bitcast.52, s32[3072]{0:T(1024)S(1)} %pad_clamp_fusion), kind=kCustom, calls=%fused_computation.1 | custom fusion | bytes 108000 | tf_op jit(solution)/shard_map/gather | solution.py:173
  295.6 3.7 collective-permute-start.33
  301.9 2.1 collective-permute-done.32
  305.1 3.5 collective-permute-start.34
  310.2 1.8 collective-permute-done.35
  312.3 1.7 fusion.47
  314.0 8.8 %copy.32 = f32[4,128,256]{0,2,1:T(8,128)} copy(f32[4,128,256]{2,1,0:T(8,128)S(1)} %fusion.47) | data formatting | bytes 1048576 | tf_op jit(solution)/shard_map/add | solution.py:85
  322.8 16.7 %gather_fusion.2 = f32[3000,4]{1,0:T(8,128)} fusion(f32[4,32768]{0,1:T(8,128)} %bitcast.51, s32[3072]{0:T(1024)S(1)} %pad_clamp_fusion), kind=kCustom, calls=%fused_computation.2 | custom fusion | bytes 108000 | tf_op jit(solution)/shard_map/gather | solution.py:186
  339.5 5.9 %fusion.3 = (f32[3000]{0:T(1024)S(1)}, f32[3000]{0:T(1024)S(1)}) fusion(f32[3000,4]{1,0:T(8,128)S(1)} %copy-done.16, f32[3000]{0:T(1024)S(1)} %subtract_add_fusion, f32[3000]{0:T(1024)S(1)} %and_convert_fusion, s32[3000]{0:T(1024)S(1)} %copy-done.18, s32[3000]{0:T(1024)S(1)} %copy-done.19, s32[4]{0:T(128)S(1)} %iota_add_fusion, ...), kind=kLoop, calls=%fused_computation.15 | loop fusion | flops 126000 | bytes 192016 | tf_op jit(solution)/shard_map/reduce_sum | solution.py:173
  345.4 67.7 %all-reduce = (f32[3000]{0:T(1024)S(1)}, f32[3000]{0:T(1024)S(1)}, f32[]{:T(128)}) all-reduce(f32[3000]{0:T(1024)S(1)} %get-tuple-element.6, f32[3000]{0:T(1024)S(1)} %get-tuple-element.5, f32[]{:T(128)} %get-tuple-element.10), channel_id=1, replica_groups=mesh['east'=4,'north'=16,'layer'=2] {'east','north','layer'}, use_global_device_ids=true, to_apply=%region_8.9 | all-reduce | flops 6001 | bytes 48008 | tf_op jit(solution)/shard_map/psum | solution.py:187
  (126 shorter events, 28.5 us)
Async XLA Ops:
  2.5 45.7 %collective-permute-start.7 = (f32[4,128,1]{2,1,0:T(8,128)}, f32[4,128,1]{2,1,0:T(8,128)S(1)}, u32[]{:S(2)}, u32[]{:S(2)}) collective-permute-start(f32[4,128,1]{2,1,0:T(8,128)} %get-tuple-element.64), channel_id=1, source_target_pairs={{0,32},{32,64},{64,96},{1,33},{33,65},{65,97},{2,34},{34,66},{66,9... | collective-permute-start | bytes 6152 | tf_op jit(solution)/shard_map/ppermute | solution.py:18
  6.6 41.7 %collective-permute-start.6 = (f32[4,128,1]{2,1,0:T(8,128)}, f32[4,128,1]{2,1,0:T(8,128)S(1)}, u32[]{:S(2)}, u32[]{:S(2)}) collective-permute-start(f32[4,128,1]{2,1,0:T(8,128)} %get-tuple-element.65), channel_id=1, source_target_pairs={{32,0},{64,32},{96,64},{33,1},{65,33},{97,65},{34,2},{66,34},{98,6... | collective-permute-start | bytes 6152 | tf_op jit(solution)/shard_map/ppermute | solution.py:19
  7.9 8.0 %copy-start.21 = (s32[3000]{0:T(1024)S(1)}, s32[3000]{0:T(1024)}, u32[]{:S(2)}) copy-start(s32[3000]{0:T(1024)} %param.20) | copy-start | bytes 36004
  7.9 7.9 %copy-start.22 = (s32[3000]{0:T(1024)S(1)}, s32[3000]{0:T(1024)}, u32[]{:S(2)}) copy-start(s32[3000]{0:T(1024)} %param.21) | copy-start | bytes 36004
  7.9 8.0 %copy-start.7 = (bf16[4,128,256]{2,1,0:T(8,128)(2,1)S(1)}, bf16[4,128,256]{2,1,0:T(8,128)(2,1)}, u32[]{:S(2)}) copy-start(bf16[4,128,256]{2,1,0:T(8,128)(2,1)} %param.16) | copy-start | bytes 786436
  10.5 31.9 %collective-permute-start = (bf16[4,4,128,1]{3,2,1,0:T(8,128)(2,1)}, bf16[4,4,128,1]{3,2,1,0:T(8,128)(2,1)S(1)}, u32[]{:S(2)}, u32[]{:S(2)}) collective-permute-start(bf16[4,4,128,1]{3,2,1,0:T(8,128)(2,1)} %get-tuple-element.52), channel_id=1, source_target_pairs={{0,32},{32,64},{64,96},{1,33},{33,65},{65,97},{2,34},{34,66},{66,9... | collective-permute-start | bytes 12296 | tf_op jit(solution)/shard_map/ppermute | solution.py:18
  14.5 27.9 %collective-permute-start.1 = (bf16[4,4,128,1]{3,2,1,0:T(8,128)(2,1)}, bf16[4,4,128,1]{3,2,1,0:T(8,128)(2,1)}, u32[]{:S(2)}, u32[]{:S(2)}) collective-permute-start(bf16[4,4,128,1]{3,2,1,0:T(8,128)(2,1)} %get-tuple-element.53), channel_id=1, source_target_pairs={{32,0},{64,32},{96,64},{33,1},{65,33},{97,65},{34,2},{66,34},{98,6... | collective-permute-start | bytes 12296 | tf_op jit(solution)/shard_map/ppermute | solution.py:19
  15.9 19.2 %copy-start.18 = (s32[3000]{0:T(1024)S(1)}, s32[3000]{0:T(1024)}, u32[]{:S(2)}) copy-start(s32[3000]{0:T(1024)} %param.23) | copy-start | bytes 36004
  15.9 19.2 %copy-start.19 = (s32[3000]{0:T(1024)S(1)}, s32[3000]{0:T(1024)}, u32[]{:S(2)}) copy-start(s32[3000]{0:T(1024)} %param.22) | copy-start | bytes 36004
  15.9 26.5 %copy-start.8 = (bf16[4,128,256]{2,1,0:T(8,128)(2,1)S(1)}, bf16[4,128,256]{2,1,0:T(8,128)(2,1)}, u32[]{:S(2)}) copy-start(bf16[4,128,256]{2,1,0:T(8,128)(2,1)} %param.19) | copy-start | bytes 786436
  15.9 26.5 %copy-start.10 = (bf16[4,128,256]{2,1,0:T(8,128)(2,1)S(1)}, bf16[4,128,256]{2,1,0:T(8,128)(2,1)}, u32[]{:S(2)}) copy-start(bf16[4,128,256]{2,1,0:T(8,128)(2,1)} %param.18) | copy-start | bytes 786436
  22.1 26.2 %copy-start = (f32[4,128,256]{2,1,0:T(8,128)S(1)}, f32[4,128,256]{2,1,0:T(8,128)}, u32[]{:S(2)}) copy-start(f32[4,128,256]{2,1,0:T(8,128)} %param.14) | copy-start | bytes 1572868
  35.1 29.0 %copy-start.4 = (bf16[3000,4]{1,0:T(8,128)(2,1)}, bf16[3000,4]{1,0:T(8,128)(2,1)S(1)}, u32[]{:S(2)}) copy-start(bf16[3000,4]{1,0:T(8,128)(2,1)S(1)} %gather_fusion) | copy-start | bytes 72004
  42.4 11.5 %copy-start.11 = (bf16[4,128,256]{2,1,0:T(8,128)(2,1)S(1)}, bf16[4,128,256]{2,1,0:T(8,128)(2,1)}, u32[]{:S(2)}) copy-start(bf16[4,128,256]{2,1,0:T(8,128)(2,1)} %param.17) | copy-start | bytes 786436
  43.4 10.5 %collective-permute-start.2 = (bf16[4,4,1,258]{3,2,1,0:T(2,128)(2,1)S(1)}, bf16[4,4,1,258]{3,2,1,0:T(2,128)(2,1)S(1)}, u32[]{:S(2)}, u32[]{:S(2)}) collective-permute-start(bf16[4,4,1,258]{3,2,1,0:T(2,128)(2,1)S(1)} %get-tuple-element.30), channel_id=1, source_target_pairs={{0,2},{2,4},{4,6},{6,8},{8,10},{10,12},{12,14},{14,16},{16,18},{18... | collective-permute-start | bytes 24776 | tf_op jit(solution)/shard_map/ppermute | solution.py:18
  47.0 6.9 %collective-permute-start.3 = (bf16[4,4,1,258]{3,2,1,0:T(2,128)(2,1)S(1)}, bf16[4,4,1,258]{3,2,1,0:T(2,128)(2,1)S(1)}, u32[]{:S(2)}, u32[]{:S(2)}) collective-permute-start(bf16[4,4,1,258]{3,2,1,0:T(2,128)(2,1)S(1)} %get-tuple-element.31), channel_id=1, source_target_pairs={{2,0},{4,2},{6,4},{8,6},{10,8},{12,10},{14,12},{16,14},{18,16},{20... | collective-permute-start | bytes 24776 | tf_op jit(solution)/shard_map/ppermute | solution.py:19
  48.4 52.7 %collective-permute-start.9 = (f32[4,1,258]{2,1,0:T(1,128)S(1)}, f32[4,1,258]{2,1,0:T(1,128)S(1)}, u32[]{:S(2)}, u32[]{:S(2)}) collective-permute-start(f32[4,1,258]{2,1,0:T(1,128)S(1)} %get-tuple-element.54), channel_id=1, source_target_pairs={{0,2},{2,4},{4,6},{6,8},{8,10},{10,12},{12,14},{14,16},{16,18},{18... | collective-permute-start | bytes 12392 | tf_op jit(solution)/shard_map/ppermute | solution.py:18
  52.6 48.5 %collective-permute-start.8 = (f32[4,1,258]{2,1,0:T(1,128)S(1)}, f32[4,1,258]{2,1,0:T(1,128)S(1)}, u32[]{:S(2)}, u32[]{:S(2)}) collective-permute-start(f32[4,1,258]{2,1,0:T(1,128)S(1)} %get-tuple-element.55), channel_id=1, source_target_pairs={{2,0},{4,2},{6,4},{8,6},{10,8},{12,10},{14,12},{16,14},{18,16},{20... | collective-permute-start | bytes 12392 | tf_op jit(solution)/shard_map/ppermute | solution.py:19
  57.3 6.8 %copy-start.20 = (f32[3000]{0:T(1024)S(1)}, f32[3000]{0:T(1024)}, u32[]{:S(2)}) copy-start(f32[3000]{0:T(1024)} %param.25) | copy-start | bytes 36004
  58.3 45.8 %collective-permute-start.4 = (bf16[4,1,130,258]{3,2,1,0:T(8,128)(2,1)}, bf16[4,1,130,258]{3,2,1,0:T(8,128)(2,1)}, u32[]{:S(2)}, u32[]{:S(2)}) collective-permute-start(bf16[4,1,130,258]{3,2,1,0:T(8,128)(2,1)} %get-tuple-element.32), channel_id=1, source_target_pairs={{0,1},{2,3},{4,5},{6,7},{8,9},{10,11},{12,13},{14,15},{16,17},{18,... | collective-permute-start | bytes 804968 | tf_op jit(solution)/shard_map/ppermute | solution.py:18
  59.6 44.5 %collective-permute-start.5 = (bf16[4,1,130,258]{3,2,1,0:T(8,128)(2,1)}, bf16[4,1,130,258]{3,2,1,0:T(8,128)(2,1)}, u32[]{:S(2)}, u32[]{:S(2)}) collective-permute-start(bf16[4,1,130,258]{3,2,1,0:T(8,128)(2,1)} %get-tuple-element.33), channel_id=1, source_target_pairs={{1,0},{3,2},{5,4},{7,6},{9,8},{11,10},{13,12},{15,14},{17,16},{19,... | collective-permute-start | bytes 804968 | tf_op jit(solution)/shard_map/ppermute | solution.py:19
  90.4 13.8 %copy-start.12 = (bf16[4,128,256]{2,1,0:T(8,128)(2,1)S(1)}, bf16[4,128,256]{2,1,0:T(8,128)(2,1)}, u32[]{:S(2)}) copy-start(bf16[4,128,256]{2,1,0:T(8,128)(2,1)} %param.17) | copy-start | bytes 786436
  101.3 9.7 %collective-permute-start.10 = (f32[1,130,258]{2,1,0:T(8,128)S(1)}, f32[1,130,258]{2,1,0:T(8,128)S(1)}, u32[]{:S(2)}, u32[]{:S(2)}) collective-permute-start(f32[1,130,258]{2,1,0:T(8,128)S(1)} %get-tuple-element.42), channel_id=1, source_target_pairs={{1,0},{3,2},{5,4},{7,6},{9,8},{11,10},{13,12},{15,14},{17,16},{19,... | collective-permute-start | bytes 402488 | tf_op jit(solution)/shard_map/ppermute | solution.py:19
  102.6 8.4 %collective-permute-start.11 = (f32[1,130,258]{2,1,0:T(8,128)S(1)}, f32[1,130,258]{2,1,0:T(8,128)S(1)}, u32[]{:S(2)}, u32[]{:S(2)}) collective-permute-start(f32[1,130,258]{2,1,0:T(8,128)S(1)} %get-tuple-element.43), channel_id=1, source_target_pairs={{0,1},{2,3},{4,5},{6,7},{8,9},{10,11},{12,13},{14,15},{16,17},{18,... | collective-permute-start | bytes 402488 | tf_op jit(solution)/shard_map/ppermute | solution.py:18
  109.9 65.5 %copy-start.6 = (f32[6,130,258]{2,1,0:T(8,128)}, f32[6,130,258]{2,1,0:T(8,128)S(1)}, u32[]{:S(2)}) copy-start(f32[6,130,258]{2,1,0:T(8,128)S(1)} %get-tuple-element.26) | copy-start | bytes 2414884
  111.0 1.0 copy-start.13
  112.1 6.3 %copy-start.24 = (s32[3000]{0:T(1024)S(1)}, s32[3000]{0:T(1024)}, u32[]{:S(2)}) copy-start(s32[3000]{0:T(1024)} %param.24) | copy-start | bytes 36004
  112.1 6.3 %copy-start.25 = (f32[4]{0:T(128)S(1)}, f32[4]{0:T(128)}, u32[]{:S(2)}) copy-start(f32[4]{0:T(128)} %param.27) | copy-start | bytes 52
  112.8 116.5 %copy-start.1 = (f32[4,128,256]{2,1,0:T(8,128)}, f32[4,128,256]{2,1,0:T(8,128)S(1)}, u32[]{:S(2)}) copy-start(f32[4,128,256]{2,1,0:T(8,128)S(1)} %get-tuple-element.19) | copy-start | bytes 1572868
  113.0 8.5 %collective-permute-start.13 = (f32[4,128,1]{2,1,0:T(8,128)S(1)}, f32[4,128,1]{2,1,0:T(8,128)S(1)}, u32[]{:S(2)}, u32[]{:S(2)}) collective-permute-start(f32[4,128,1]{2,1,0:T(8,128)S(1)} %get-tuple-element.62), channel_id=1, source_target_pairs={{0,32},{32,64},{64,96},{1,33},{33,65},{65,97},{2,34},{34,66},{66,9... | collective-permute-start | bytes 6152 | tf_op jit(solution)/shard_map/ppermute | solution.py:18
  117.1 8.3 %collective-permute-start.12 = (f32[4,128,1]{2,1,0:T(8,128)S(1)}, f32[4,128,1]{2,1,0:T(8,128)S(1)}, u32[]{:S(2)}, u32[]{:S(2)}) collective-permute-start(f32[4,128,1]{2,1,0:T(8,128)S(1)} %get-tuple-element.63), channel_id=1, source_target_pairs={{32,0},{64,32},{96,64},{33,1},{65,33},{97,65},{34,2},{66,34},{98,6... | collective-permute-start | bytes 6152 | tf_op jit(solution)/shard_map/ppermute | solution.py:19
  125.5 5.6 %collective-permute-start.15 = (f32[4,1,258]{2,1,0:T(1,128)S(1)}, f32[4,1,258]{2,1,0:T(1,128)S(1)}, u32[]{:S(2)}, u32[]{:S(2)}) collective-permute-start(f32[4,1,258]{2,1,0:T(1,128)S(1)} %get-tuple-element.50), channel_id=1, source_target_pairs={{0,2},{2,4},{4,6},{6,8},{8,10},{10,12},{12,14},{14,16},{16,18},{18... | collective-permute-start | bytes 12392 | tf_op jit(solution)/shard_map/ppermute | solution.py:18
  129.5 4.5 %collective-permute-start.14 = (f32[4,1,258]{2,1,0:T(1,128)S(1)}, f32[4,1,258]{2,1,0:T(1,128)S(1)}, u32[]{:S(2)}, u32[]{:S(2)}) collective-permute-start(f32[4,1,258]{2,1,0:T(1,128)S(1)} %get-tuple-element.51), channel_id=1, source_target_pairs={{2,0},{4,2},{6,4},{8,6},{10,8},{12,10},{14,12},{16,14},{18,16},{20... | collective-permute-start | bytes 12392 | tf_op jit(solution)/shard_map/ppermute | solution.py:19
  134.2 7.1 %collective-permute-start.16 = (f32[1,130,258]{2,1,0:T(8,128)S(1)}, f32[1,130,258]{2,1,0:T(8,128)S(1)}, u32[]{:S(2)}, u32[]{:S(2)}) collective-permute-start(f32[1,130,258]{2,1,0:T(8,128)S(1)} %get-tuple-element.40), channel_id=1, source_target_pairs={{1,0},{3,2},{5,4},{7,6},{9,8},{11,10},{13,12},{15,14},{17,16},{19,... | collective-permute-start | bytes 402488 | tf_op jit(solution)/shard_map/ppermute | solution.py:19
  139.7 3.4 collective-permute-start.17
  144.1 9.1 %collective-permute-start.19 = (f32[4,128,1]{2,1,0:T(8,128)S(1)}, f32[4,128,1]{2,1,0:T(8,128)S(1)}, u32[]{:S(2)}, u32[]{:S(2)}) collective-permute-start(f32[4,128,1]{2,1,0:T(8,128)S(1)} %get-tuple-element.60), channel_id=1, source_target_pairs={{0,32},{32,64},{64,96},{1,33},{33,65},{65,97},{2,34},{34,66},{66,9... | collective-permute-start | bytes 6152 | tf_op jit(solution)/shard_map/ppermute | solution.py:18
  147.6 9.3 %collective-permute-start.18 = (f32[4,128,1]{2,1,0:T(8,128)S(1)}, f32[4,128,1]{2,1,0:T(8,128)S(1)}, u32[]{:S(2)}, u32[]{:S(2)}) collective-permute-start(f32[4,128,1]{2,1,0:T(8,128)S(1)} %get-tuple-element.61), channel_id=1, source_target_pairs={{32,0},{64,32},{96,64},{33,1},{65,33},{97,65},{34,2},{66,34},{98,6... | collective-permute-start | bytes 6152 | tf_op jit(solution)/shard_map/ppermute | solution.py:19
  157.1 5.2 %collective-permute-start.21 = (f32[4,1,258]{2,1,0:T(1,128)S(1)}, f32[4,1,258]{2,1,0:T(1,128)S(1)}, u32[]{:S(2)}, u32[]{:S(2)}) collective-permute-start(f32[4,1,258]{2,1,0:T(1,128)S(1)} %get-tuple-element.48), channel_id=1, source_target_pairs={{0,2},{2,4},{4,6},{6,8},{8,10},{10,12},{12,14},{14,16},{16,18},{18... | collective-permute-start | bytes 12392 | tf_op jit(solution)/shard_map/ppermute | solution.py:18
  160.6 6.5 %collective-permute-start.20 = (f32[4,1,258]{2,1,0:T(1,128)S(1)}, f32[4,1,258]{2,1,0:T(1,128)S(1)}, u32[]{:S(2)}, u32[]{:S(2)}) collective-permute-start(f32[4,1,258]{2,1,0:T(1,128)S(1)} %get-tuple-element.49), channel_id=1, source_target_pairs={{2,0},{4,2},{6,4},{8,6},{10,8},{12,10},{14,12},{16,14},{18,16},{20... | collective-permute-start | bytes 12392 | tf_op jit(solution)/shard_map/ppermute | solution.py:19
  167.4 6.1 %collective-permute-start.22 = (f32[1,130,258]{2,1,0:T(8,128)S(1)}, f32[1,130,258]{2,1,0:T(8,128)S(1)}, u32[]{:S(2)}, u32[]{:S(2)}) collective-permute-start(f32[1,130,258]{2,1,0:T(8,128)S(1)} %get-tuple-element.38), channel_id=1, source_target_pairs={{1,0},{3,2},{5,4},{7,6},{9,8},{11,10},{13,12},{15,14},{17,16},{19,... | collective-permute-start | bytes 402488 | tf_op jit(solution)/shard_map/ppermute | solution.py:19
  171.7 3.4 collective-permute-start.23
  173.5 1.9 copy-start.17
  230.6 8.6 %collective-permute-start.25 = (f32[4,128,1]{2,1,0:T(8,128)S(1)}, f32[4,128,1]{2,1,0:T(8,128)S(1)}, u32[]{:S(2)}, u32[]{:S(2)}) collective-permute-start(f32[4,128,1]{2,1,0:T(8,128)S(1)} %get-tuple-element.58), channel_id=1, source_target_pairs={{0,32},{32,64},{64,96},{1,33},{33,65},{65,97},{2,34},{34,66},{66,9... | collective-permute-start | bytes 6152 | tf_op jit(solution)/shard_map/ppermute | solution.py:18
  233.8 9.2 %collective-permute-start.24 = (f32[4,128,1]{2,1,0:T(8,128)S(1)}, f32[4,128,1]{2,1,0:T(8,128)S(1)}, u32[]{:S(2)}, u32[]{:S(2)}) collective-permute-start(f32[4,128,1]{2,1,0:T(8,128)S(1)} %get-tuple-element.59), channel_id=1, source_target_pairs={{32,0},{64,32},{96,64},{33,1},{65,33},{97,65},{34,2},{66,34},{98,6... | collective-permute-start | bytes 6152 | tf_op jit(solution)/shard_map/ppermute | solution.py:19
  243.1 7.4 %collective-permute-start.27 = (f32[4,1,258]{2,1,0:T(1,128)S(1)}, f32[4,1,258]{2,1,0:T(1,128)S(1)}, u32[]{:S(2)}, u32[]{:S(2)}) collective-permute-start(f32[4,1,258]{2,1,0:T(1,128)S(1)} %get-tuple-element.46), channel_id=1, source_target_pairs={{0,2},{2,4},{4,6},{6,8},{8,10},{10,12},{12,14},{14,16},{16,18},{18... | collective-permute-start | bytes 12392 | tf_op jit(solution)/shard_map/ppermute | solution.py:18
  248.9 4.7 %collective-permute-start.26 = (f32[4,1,258]{2,1,0:T(1,128)S(1)}, f32[4,1,258]{2,1,0:T(1,128)S(1)}, u32[]{:S(2)}, u32[]{:S(2)}) collective-permute-start(f32[4,1,258]{2,1,0:T(1,128)S(1)} %get-tuple-element.47), channel_id=1, source_target_pairs={{2,0},{4,2},{6,4},{8,6},{10,8},{12,10},{14,12},{16,14},{18,16},{20... | collective-permute-start | bytes 12392 | tf_op jit(solution)/shard_map/ppermute | solution.py:19
  253.8 6.0 %collective-permute-start.28 = (f32[1,130,258]{2,1,0:T(8,128)S(1)}, f32[1,130,258]{2,1,0:T(8,128)S(1)}, u32[]{:S(2)}, u32[]{:S(2)}) collective-permute-start(f32[1,130,258]{2,1,0:T(8,128)S(1)} %get-tuple-element.36), channel_id=1, source_target_pairs={{1,0},{3,2},{5,4},{7,6},{9,8},{11,10},{13,12},{15,14},{17,16},{19,... | collective-permute-start | bytes 402488 | tf_op jit(solution)/shard_map/ppermute | solution.py:19
  258.2 3.4 collective-permute-start.29
  259.8 2.1 copy-start.2
  259.8 2.1 copy-start.9
  265.3 29.5 %collective-permute-start.31 = (f32[4,128,1]{2,1,0:T(8,128)}, f32[4,128,1]{2,1,0:T(8,128)S(1)}, u32[]{:S(2)}, u32[]{:S(2)}) collective-permute-start(f32[4,128,1]{2,1,0:T(8,128)} %get-tuple-element.56), channel_id=1, source_target_pairs={{0,32},{32,64},{64,96},{1,33},{33,65},{65,97},{2,34},{34,66},{66,9... | collective-permute-start | bytes 6152 | tf_op jit(solution)/shard_map/ppermute | solution.py:18
  267.2 27.6 %collective-permute-start.30 = (f32[4,128,1]{2,1,0:T(8,128)}, f32[4,128,1]{2,1,0:T(8,128)}, u32[]{:S(2)}, u32[]{:S(2)}) collective-permute-start(f32[4,128,1]{2,1,0:T(8,128)} %get-tuple-element.57), channel_id=1, source_target_pairs={{32,0},{64,32},{96,64},{33,1},{65,33},{97,65},{34,2},{66,34},{98,6... | collective-permute-start | bytes 6152 | tf_op jit(solution)/shard_map/ppermute | solution.py:19
  295.6 6.3 %collective-permute-start.33 = (f32[4,1,258]{2,1,0:T(1,128)S(1)}, f32[4,1,258]{2,1,0:T(1,128)S(1)}, u32[]{:S(2)}, u32[]{:S(2)}) collective-permute-start(f32[4,1,258]{2,1,0:T(1,128)S(1)} %get-tuple-element.44), channel_id=1, source_target_pairs={{0,2},{2,4},{4,6},{6,8},{8,10},{10,12},{12,14},{14,16},{16,18},{18... | collective-permute-start | bytes 12392 | tf_op jit(solution)/shard_map/ppermute | solution.py:18
  299.3 4.7 %collective-permute-start.32 = (f32[4,1,258]{2,1,0:T(1,128)S(1)}, f32[4,1,258]{2,1,0:T(1,128)S(1)}, u32[]{:S(2)}, u32[]{:S(2)}) collective-permute-start(f32[4,1,258]{2,1,0:T(1,128)S(1)} %get-tuple-element.45), channel_id=1, source_target_pairs={{2,0},{4,2},{6,4},{8,6},{10,8},{12,10},{14,12},{16,14},{18,16},{20... | collective-permute-start | bytes 12392 | tf_op jit(solution)/shard_map/ppermute | solution.py:19
  305.1 5.1 %collective-permute-start.34 = (f32[1,130,258]{2,1,0:T(8,128)S(1)}, f32[1,130,258]{2,1,0:T(8,128)S(1)}, u32[]{:S(2)}, u32[]{:S(2)}) collective-permute-start(f32[1,130,258]{2,1,0:T(8,128)S(1)} %get-tuple-element.34), channel_id=1, source_target_pairs={{1,0},{3,2},{5,4},{7,6},{9,8},{11,10},{13,12},{15,14},{17,16},{19,... | collective-permute-start | bytes 402488 | tf_op jit(solution)/shard_map/ppermute | solution.py:19
  308.6 3.4 collective-permute-start.35
  310.2 2.1 copy-start.3
  310.2 2.1 copy-start.14
  314.0 8.8 %copy-start.15 = (f32[4,128,256]{2,1,0:T(8,128)}, f32[4,128,256]{2,1,0:T(8,128)S(1)}, u32[]{:S(2)}) copy-start(f32[4,128,256]{2,1,0:T(8,128)S(1)} %fusion.47) | copy-start | bytes 1572868
  314.0 25.5 %copy-start.5 = (bf16[3000,4]{1,0:T(8,128)(2,1)S(1)}, bf16[3000,4]{1,0:T(8,128)(2,1)}, u32[]{:S(2)}) copy-start(bf16[3000,4]{1,0:T(8,128)(2,1)} %copy-done.4) | copy-start | bytes 72004
  314.0 25.5 %copy-start.16 = (f32[3000,4]{1,0:T(8,128)S(1)}, f32[3000,4]{1,0:T(8,128)}, u32[]{:S(2)}) copy-start(f32[3000,4]{1,0:T(8,128)} %gather_fusion.1) | copy-start | bytes 144004
  339.5 74.3 %copy-start.23 = (f32[3000]{0:T(1024)S(1)}, f32[3000]{0:T(1024)}, u32[]{:S(2)}) copy-start(f32[3000]{0:T(1024)} %param.26) | copy-start | bytes 36004
where the time goes:
time: 419 us; the launch traced here: 416 us
  local copies, waits for them, and re-layouts  108 us (26%)
  other arithmetic  96.3 us (23%)
  starting transfers between devices  92.9 us (22%)
  blocking collectives  72.3 us (17%)
  waiting for transfers between devices  42.8 us (10%)
    psum x1, blocking collectives, per_device(): adjoint_screen = lax.psum(adjoint_part, ('east', 'north', 'layer'))  67.7 us
    ppermute x18, starting transfers between devices, extended(): before = lax.ppermute(last, axis, up)  53.7 us
    ppermute x18, starting transfers between devices, extended(): after = lax.ppermute(initial, axis, down)  39.2 us
    scatter-add x1, other arithmetic, per_device(): load = departure.reshape(flat_shape).at[:, cells].add(-(prices * pump_rat...  31.2 us
    scatter-add x1, other arithmetic, per_device(): source = jnp.zeros(flat_shape, jnp.float32).at[:, cells].add(pump_rates[N...  26.2 us
    ppermute x18, waiting for transfers between devices, extended(): after = lax.ppermute(initial, axis, down)  24.5 us
    add x2, local copies, waits for them, and re-layouts, chebyshev(): iterate = trim(iterate) + direction  18.4 us
    ppermute x18, waiting for transfers between devices, extended(): before = lax.ppermute(last, axis, up)  18.3 us
  transfers between devices with their start and end apart: 36, of which 14 were waited for; matrix products, arithmetic and copies ran while one was open for 25% of the time, Pallas kernels for 0%

commit v1 on v0

--- a/solution.py
+++ b/solution.py
@@ -184,7 +184,7 @@
     )
     adjoint_head = chebyshev(None, load, operate, keep_whole, precondition)
     adjoint_part = jnp.sum(shares * adjoint_head.reshape(flat_shape)[:, cells], axis=0)
-    adjoint_screen = lax.psum(adjoint_part, ("east", "north", "layer"))
+    adjoint_screen = lax.psum(lax.psum(adjoint_part, "east"), ("north", "layer"))
     misfit = misfit_total / all_cells
     lift = ground_level - head_screen
     rate_gradient = prices * lift - adjoint_screen

time: 419 us -> 553 us (1.32)
  blocking collectives: 72.3 us -> 207 us
    psum x1 -> x3, blocking collectives: 67.7 us -> 202 us  [the longest x1 122 us: per_device(): lax.psum(lax.psum(adjoint_part, 'east'), ('north', 'layer'))]
  transfers between devices with their start and end apart: 36 -> 36, of which waited for: 14 -> 14; matrix products, arithmetic and copies ran while one was open for 25% -> 19% of each run, Pallas kernels for 0% -> 0%
where the time goes in v1:
time: 553 us; the launch traced here: 551 us
  blocking collectives  207 us (37%)
  local copies, waits for them, and re-layouts  108 us (20%)
  other arithmetic  96.3 us (17%)
  starting transfers between devices  92.9 us (17%)
  waiting for transfers between devices  42.8 us (8%)
    psum x1, blocking collectives, per_device(): lax.psum(lax.psum(adjoint_part, 'east'), ('north', 'layer'))  122 us
    psum x1, blocking collectives, per_device(): lax.psum((head_part, misfit_part), ('east', 'north', 'layer'))  67.4 us
    ppermute x18, starting transfers between devices, extended(): before = lax.ppermute(last, axis, up)  53.7 us
    ppermute x18, starting transfers between devices, extended(): after = lax.ppermute(initial, axis, down)  39.2 us
    scatter-add x1, other arithmetic, per_device(): load = departure.reshape(flat_shape).at[:, cells].add(-(prices * pump_rat...  31.2 us
    scatter-add x1, other arithmetic, per_device(): source = jnp.zeros(flat_shape, jnp.float32).at[:, cells].add(pump_rates[N...  26.2 us
    ppermute x18, waiting for transfers between devices, extended(): after = lax.ppermute(initial, axis, down)  24.5 us
    add x2, local copies, waits for them, and re-layouts, chebyshev(): iterate = trim(iterate) + direction  18.5 us
  transfers between devices with their start and end apart: 36, of which 14 were waited for; matrix products, arithmetic and copies ran while one was open for 19% of the time, Pallas kernels for 0%

profile of v1, /device:TPU:1, one launch (start us, length us, event | category | flops | bytes accessed | tf_op | source)
XLA Modules:
  0.0 550.9 jit_solution(9204657253975425472)
XLA Ops:
  0.6 1.9 fusion.86
  2.5 4.0 collective-permute-start.7
  6.6 1.3 collective-permute-start.6
  7.9 1.4 pad_maximum_fusion.1
  10.5 4.0 collective-permute-start
  14.5 1.3 collective-permute-start.1
  15.9 6.2 %copy.26 = bf16[4,128,256]{0,2,1:T(8,128)(2,1)} copy(bf16[4,128,256]{2,1,0:T(8,128)(2,1)S(1)} %copy-done.7) | data formatting | bytes 524288 | tf_op args[2]
  22.1 13.0 %gather_fusion = bf16[3000,4]{1,0:T(8,128)(2,1)S(1)} fusion(bf16[4,32768]{0,1:T(8,128)(2,1)} %bitcast.53, s32[3072]{0:T(1024)S(1)} %pad_clamp_fusion), kind=kCustom, calls=%fused_computation | custom fusion | bytes 60000 | tf_op jit(solution)/shard_map/gather | solution.py:146
  35.2 2.6 fusion.10
  37.8 4.6 psum.35
  43.5 3.5 collective-permute-start.2
  47.0 1.3 collective-permute-start.3
  48.5 4.2 collective-permute-start.9
  54.0 3.4 pad_maximum_fusion
  59.6 4.5 collective-permute-start.5
  64.2 26.2 %scatter_custom_fusion = f32[4,32768]{0,1:T(8,128)} fusion(s32[3000]{0:T(1024)S(1)} %compare_select_fusion.5, f32[]{:T(128)} %constant.20.clone.1, f32[3000]{0:T(1024)S(1)} %copy-done.20, bf16[3000,4]{1,0:T(8,128)(2,1)S(1)} %gather_fusion, f32[3000]{0:T(1024)S(1)} %subtract_add_fusion, f32[3000]{0:T(1024)S(1)} %and_convert_fusion, s32[4]{0:T(128)S(1)} %iota_add_fusion, ...), kind=kCustom, calls=%fused_computation.5 | custom fusion | flops 108000 | bytes 1354244 | tf_op jit(solution)/shard_map/scatter-add | solution.py:157
  90.4 10.7 %copy.27 = f32[4,128,256]{2,1,0:T(8,128)} copy(f32[4,128,256]{0,2,1:T(8,128)} %bitcast.50) | data formatting | bytes 1048576 | tf_op jit(solution)/shard_map/reshape | solution.py:158
  101.4 1.3 collective-permute-start.10
  102.7 1.5 collective-permute-start.11
  104.2 5.4 maximum_convert_fusion
  113.0 4.1 collective-permute-start.13
  117.1 1.3 collective-permute-start.12
  118.6 3.0 collective-permute-done.13
  121.6 3.8 collective-permute-done.12
  125.5 4.0 collective-permute-start.15
  131.1 2.9 collective-permute-done.14
  134.3 5.5 %collective-permute-start.16 = (f32[1,130,258]{2,1,0:T(8,128)S(1)}, f32[1,130,258]{2,1,0:T(8,128)S(1)}, u32[]{:S(2)}, u32[]{:S(2)}) collective-permute-start(f32[1,130,258]{2,1,0:T(8,128)S(1)} %get-tuple-element.39), channel_id=1, source_target_pairs={{1,0},{3,2},{5,4},{7,6},{9,8},{11,10},{13,12},{15,14},{17,16},{19,... | collective-permute-start | bytes 402488 | tf_op jit(solution)/shard_map/ppermute | solution.py:19
  141.3 1.8 collective-permute-done.17
  144.1 3.6 collective-permute-start.19
  149.0 4.2 collective-permute-done.19
  153.2 3.8 collective-permute-done.18
  157.1 3.6 collective-permute-start.21
  162.3 4.9 collective-permute-done.20
  167.4 4.3 collective-permute-start.22
  171.7 1.5 collective-permute-start.23
  173.5 1.6 collective-permute-done.23
  175.4 2.2 multiply_reduce_fusion
  177.6 9.8 %copy.28 = f32[4,128,256]{0,2,1:T(8,128)} copy(f32[4,128,256]{2,1,0:T(8,128)} %get-tuple-element.10) | data formatting | bytes 1048576 | tf_op jit(solution)/shard_map/sub | solution.py:163
  187.4 31.2 %scatter_custom_fusion.1 = f32[4,32768]{0,1:T(8,128)} fusion(f32[4,32768]{0,1:T(8,128)} %bitcast.48, s32[3000]{0:T(1024)S(1)} %compare_select_fusion.5, f32[3000]{0:T(1024)S(1)} %multiply_negate_fusion, bf16[3000,4]{1,0:T(8,128)(2,1)} %copy-done.4, f32[3000]{0:T(1024)S(1)} %subtract_add_fusion, f32[3000]{0:T(1024)S(1)} %and_convert_fusion, ...), kind=kCustom, calls=%fused_computation.16 | custom fusion | flops 108000 | bytes 1354240 | tf_op jit(solution)/shard_map/scatter-add | solution.py:182
  218.7 10.7 %copy.29 = f32[4,128,256]{2,1,0:T(8,128)} copy(f32[4,128,256]{0,2,1:T(8,128)} %bitcast.49) | data formatting | bytes 1048576 | tf_op jit(solution)/shard_map/reshape | solution.py:183
  230.6 3.2 collective-permute-start.25
  235.1 4.1 collective-permute-done.25
  239.2 3.8 collective-permute-done.24
  243.1 5.7 %collective-permute-start.27 = (f32[4,1,258]{2,1,0:T(1,128)S(1)}, f32[4,1,258]{2,1,0:T(1,128)S(1)}, u32[]{:S(2)}, u32[]{:S(2)}) collective-permute-start(f32[4,1,258]{2,1,0:T(1,128)S(1)} %get-tuple-element.45), channel_id=1, source_target_pairs={{0,2},{2,4},{4,6},{6,8},{8,10},{10,12},{12,14},{14,16},{16,18},{18... | collective-permute-start | bytes 12392 | tf_op jit(solution)/shard_map/ppermute | solution.py:18
  250.5 3.1 collective-permute-done.26
  253.8 4.5 collective-permute-start.28
  258.2 1.3 collective-permute-start.29
  259.8 1.8 collective-permute-done.29
  261.9 2.5 multiply_add_fusion
  265.3 1.9 collective-permute-start.31
  268.5 9.7 %copy.31 = f32[4,128,256]{0,2,1:T(8,128)} copy(f32[4,128,256]{2,1,0:T(8,128)} %get-tuple-element.11) | data formatting | bytes 1048576 | tf_op jit(solution)/shard_map/add | solution.py:85
  278.2 16.6 %gather_fusion.1 = f32[3000,4]{1,0:T(8,128)} fusion(f32[4,32768]{0,1:T(8,128)} %bitcast.52, s32[3072]{0:T(1024)S(1)} %pad_clamp_fusion), kind=kCustom, calls=%fused_computation.1 | custom fusion | bytes 108000 | tf_op jit(solution)/shard_map/gather | solution.py:173
  295.7 3.7 collective-permute-start.33
  299.4 1.3 collective-permute-start.32
  302.0 2.1 collective-permute-done.32
  305.2 3.5 collective-permute-start.34
  310.3 1.8 collective-permute-done.35
  312.4 1.7 fusion.47
  314.1 8.7 %copy.32 = f32[4,128,256]{0,2,1:T(8,128)} copy(f32[4,128,256]{2,1,0:T(8,128)S(1)} %fusion.47) | data formatting | bytes 1048576 | tf_op jit(solution)/shard_map/add | solution.py:85
  322.9 16.7 %gather_fusion.2 = f32[3000,4]{1,0:T(8,128)} fusion(f32[4,32768]{0,1:T(8,128)} %bitcast.51, s32[3072]{0:T(1024)S(1)} %pad_clamp_fusion), kind=kCustom, calls=%fused_computation.2 | custom fusion | bytes 108000 | tf_op jit(solution)/shard_map/gather | solution.py:186
  339.5 5.9 %fusion.3 = (f32[3000]{0:T(1024)S(1)}, f32[3000]{0:T(1024)S(1)}) fusion(f32[3000,4]{1,0:T(8,128)S(1)} %copy-done.16, f32[3000]{0:T(1024)S(1)} %subtract_add_fusion, f32[3000]{0:T(1024)S(1)} %and_convert_fusion, s32[3000]{0:T(1024)S(1)} %copy-done.18, s32[3000]{0:T(1024)S(1)} %copy-done.19, s32[4]{0:T(128)S(1)} %iota_add_fusion, ...), kind=kLoop, calls=%fused_computation.15 | loop fusion | flops 126000 | bytes 192016 | tf_op jit(solution)/shard_map/reduce_sum | solution.py:173
  345.5 13.0 %psum.37 = f32[3000]{0:T(1024)S(1)} all-reduce(f32[3000]{0:T(1024)S(1)} %get-tuple-element.6), channel_id=1, replica_groups=mesh['east'=4,'north'=16,'layer'=2] {'east'}, use_global_device_ids=true, to_apply=%region_8.9 | all-reduce | flops 3000 | bytes 24000 | tf_op jit(solution)/shard_map/psum | solution.py:187
  358.4 122.1 %psum.38 = f32[3000]{0:T(1024)S(1)} all-reduce(f32[3000]{0:T(1024)S(1)} %psum.37), channel_id=1, replica_groups=mesh['east'=4,'north'=16,'layer'=2] {'north','layer'}, use_global_device_ids=true, to_apply=%region_9.10 | all-reduce | flops 3000 | bytes 24000 | tf_op jit(solution)/shard_map/psum | solution.py:187
  480.5 67.4 %all-reduce = (f32[3000]{0:T(1024)S(1)}, f32[]{:T(128)}) all-reduce(f32[3000]{0:T(1024)S(1)} %get-tuple-element.5, f32[]{:T(128)} %get-tuple-element.9), channel_id=1, replica_groups=mesh['east'=4,'north'=16,'layer'=2] {'east','north','layer'}, use_global_device_ids=true, to_apply=%region_6.7 | all-reduce | flops 3001 | bytes 24008 | tf_op jit(solution)/shard_map/psum | solution.py:174
  (128 shorter events, 31.1 us)
Async XLA Ops:
  2.5 45.8 %collective-permute-start.7 = (f32[4,128,1]{2,1,0:T(8,128)}, f32[4,128,1]{2,1,0:T(8,128)S(1)}, u32[]{:S(2)}, u32[]{:S(2)}) collective-permute-start(f32[4,128,1]{2,1,0:T(8,128)} %get-tuple-element.63), channel_id=1, source_target_pairs={{0,32},{32,64},{64,96},{1,33},{33,65},{65,97},{2,34},{34,66},{66,9... | collective-permute-start | bytes 6152 | tf_op jit(solution)/shard_map/ppermute | solution.py:18
  6.6 41.8 %collective-permute-start.6 = (f32[4,128,1]{2,1,0:T(8,128)}, f32[4,128,1]{2,1,0:T(8,128)S(1)}, u32[]{:S(2)}, u32[]{:S(2)}) collective-permute-start(f32[4,128,1]{2,1,0:T(8,128)} %get-tuple-element.64), channel_id=1, source_target_pairs={{32,0},{64,32},{96,64},{33,1},{65,33},{97,65},{34,2},{66,34},{98,6... | collective-permute-start | bytes 6152 | tf_op jit(solution)/shard_map/ppermute | solution.py:19
  7.9 8.0 %copy-start.21 = (s32[3000]{0:T(1024)S(1)}, s32[3000]{0:T(1024)}, u32[]{:S(2)}) copy-start(s32[3000]{0:T(1024)} %param.20) | copy-start | bytes 36004
  7.9 8.0 %copy-start.22 = (s32[3000]{0:T(1024)S(1)}, s32[3000]{0:T(1024)}, u32[]{:S(2)}) copy-start(s32[3000]{0:T(1024)} %param.21) | copy-start | bytes 36004
  7.9 8.0 %copy-start.7 = (bf16[4,128,256]{2,1,0:T(8,128)(2,1)S(1)}, bf16[4,128,256]{2,1,0:T(8,128)(2,1)}, u32[]{:S(2)}) copy-start(bf16[4,128,256]{2,1,0:T(8,128)(2,1)} %param.16) | copy-start | bytes 786436
  10.5 32.0 %collective-permute-start = (bf16[4,4,128,1]{3,2,1,0:T(8,128)(2,1)}, bf16[4,4,128,1]{3,2,1,0:T(8,128)(2,1)S(1)}, u32[]{:S(2)}, u32[]{:S(2)}) collective-permute-start(bf16[4,4,128,1]{3,2,1,0:T(8,128)(2,1)} %get-tuple-element.51), channel_id=1, source_target_pairs={{0,32},{32,64},{64,96},{1,33},{33,65},{65,97},{2,34},{34,66},{66,9... | collective-permute-start | bytes 12296 | tf_op jit(solution)/shard_map/ppermute | solution.py:18
  14.5 28.0 %collective-permute-start.1 = (bf16[4,4,128,1]{3,2,1,0:T(8,128)(2,1)}, bf16[4,4,128,1]{3,2,1,0:T(8,128)(2,1)}, u32[]{:S(2)}, u32[]{:S(2)}) collective-permute-start(bf16[4,4,128,1]{3,2,1,0:T(8,128)(2,1)} %get-tuple-element.52), channel_id=1, source_target_pairs={{32,0},{64,32},{96,64},{33,1},{65,33},{97,65},{34,2},{66,34},{98,6... | collective-permute-start | bytes 12296 | tf_op jit(solution)/shard_map/ppermute | solution.py:19
  15.9 19.3 %copy-start.18 = (s32[3000]{0:T(1024)S(1)}, s32[3000]{0:T(1024)}, u32[]{:S(2)}) copy-start(s32[3000]{0:T(1024)} %param.23) | copy-start | bytes 36004
  15.9 19.3 %copy-start.19 = (s32[3000]{0:T(1024)S(1)}, s32[3000]{0:T(1024)}, u32[]{:S(2)}) copy-start(s32[3000]{0:T(1024)} %param.22) | copy-start | bytes 36004
  15.9 26.6 %copy-start.8 = (bf16[4,128,256]{2,1,0:T(8,128)(2,1)S(1)}, bf16[4,128,256]{2,1,0:T(8,128)(2,1)}, u32[]{:S(2)}) copy-start(bf16[4,128,256]{2,1,0:T(8,128)(2,1)} %param.19) | copy-start | bytes 786436
  15.9 26.6 %copy-start.10 = (bf16[4,128,256]{2,1,0:T(8,128)(2,1)S(1)}, bf16[4,128,256]{2,1,0:T(8,128)(2,1)}, u32[]{:S(2)}) copy-start(bf16[4,128,256]{2,1,0:T(8,128)(2,1)} %param.18) | copy-start | bytes 786436
  22.1 26.2 %copy-start = (f32[4,128,256]{2,1,0:T(8,128)S(1)}, f32[4,128,256]{2,1,0:T(8,128)}, u32[]{:S(2)}) copy-start(f32[4,128,256]{2,1,0:T(8,128)} %param.14) | copy-start | bytes 1572868
  35.2 29.0 %copy-start.4 = (bf16[3000,4]{1,0:T(8,128)(2,1)}, bf16[3000,4]{1,0:T(8,128)(2,1)S(1)}, u32[]{:S(2)}) copy-start(bf16[3000,4]{1,0:T(8,128)(2,1)S(1)} %gather_fusion) | copy-start | bytes 72004
  42.5 11.5 %copy-start.11 = (bf16[4,128,256]{2,1,0:T(8,128)(2,1)S(1)}, bf16[4,128,256]{2,1,0:T(8,128)(2,1)}, u32[]{:S(2)}) copy-start(bf16[4,128,256]{2,1,0:T(8,128)(2,1)} %param.17) | copy-start | bytes 786436
  43.5 10.5 %collective-permute-start.2 = (bf16[4,4,1,258]{3,2,1,0:T(2,128)(2,1)S(1)}, bf16[4,4,1,258]{3,2,1,0:T(2,128)(2,1)S(1)}, u32[]{:S(2)}, u32[]{:S(2)}) collective-permute-start(bf16[4,4,1,258]{3,2,1,0:T(2,128)(2,1)S(1)} %get-tuple-element.29), channel_id=1, source_target_pairs={{0,2},{2,4},{4,6},{6,8},{8,10},{10,12},{12,14},{14,16},{16,18},{18... | collective-permute-start | bytes 24776 | tf_op jit(solution)/shard_map/ppermute | solution.py:18
  47.0 6.9 %collective-permute-start.3 = (bf16[4,4,1,258]{3,2,1,0:T(2,128)(2,1)S(1)}, bf16[4,4,1,258]{3,2,1,0:T(2,128)(2,1)S(1)}, u32[]{:S(2)}, u32[]{:S(2)}) collective-permute-start(bf16[4,4,1,258]{3,2,1,0:T(2,128)(2,1)S(1)} %get-tuple-element.30), channel_id=1, source_target_pairs={{2,0},{4,2},{6,4},{8,6},{10,8},{12,10},{14,12},{16,14},{18,16},{20... | collective-permute-start | bytes 24776 | tf_op jit(solution)/shard_map/ppermute | solution.py:19
  48.5 52.7 %collective-permute-start.9 = (f32[4,1,258]{2,1,0:T(1,128)S(1)}, f32[4,1,258]{2,1,0:T(1,128)S(1)}, u32[]{:S(2)}, u32[]{:S(2)}) collective-permute-start(f32[4,1,258]{2,1,0:T(1,128)S(1)} %get-tuple-element.53), channel_id=1, source_target_pairs={{0,2},{2,4},{4,6},{6,8},{8,10},{10,12},{12,14},{14,16},{16,18},{18... | collective-permute-start | bytes 12392 | tf_op jit(solution)/shard_map/ppermute | solution.py:18
  52.6 48.5 %collective-permute-start.8 = (f32[4,1,258]{2,1,0:T(1,128)S(1)}, f32[4,1,258]{2,1,0:T(1,128)S(1)}, u32[]{:S(2)}, u32[]{:S(2)}) collective-permute-start(f32[4,1,258]{2,1,0:T(1,128)S(1)} %get-tuple-element.54), channel_id=1, source_target_pairs={{2,0},{4,2},{6,4},{8,6},{10,8},{12,10},{14,12},{16,14},{18,16},{20... | collective-permute-start | bytes 12392 | tf_op jit(solution)/shard_map/ppermute | solution.py:19
  57.3 6.8 %copy-start.20 = (f32[3000]{0:T(1024)S(1)}, f32[3000]{0:T(1024)}, u32[]{:S(2)}) copy-start(f32[3000]{0:T(1024)} %param.25) | copy-start | bytes 36004
  58.3 45.8 %collective-permute-start.4 = (bf16[4,1,130,258]{3,2,1,0:T(8,128)(2,1)}, bf16[4,1,130,258]{3,2,1,0:T(8,128)(2,1)}, u32[]{:S(2)}, u32[]{:S(2)}) collective-permute-start(bf16[4,1,130,258]{3,2,1,0:T(8,128)(2,1)} %get-tuple-element.31), channel_id=1, source_target_pairs={{0,1},{2,3},{4,5},{6,7},{8,9},{10,11},{12,13},{14,15},{16,17},{18,... | collective-permute-start | bytes 804968 | tf_op jit(solution)/shard_map/ppermute | solution.py:18
  59.6 44.5 %collective-permute-start.5 = (bf16[4,1,130,258]{3,2,1,0:T(8,128)(2,1)}, bf16[4,1,130,258]{3,2,1,0:T(8,128)(2,1)}, u32[]{:S(2)}, u32[]{:S(2)}) collective-permute-start(bf16[4,1,130,258]{3,2,1,0:T(8,128)(2,1)} %get-tuple-element.32), channel_id=1, source_target_pairs={{1,0},{3,2},{5,4},{7,6},{9,8},{11,10},{13,12},{15,14},{17,16},{19,... | collective-permute-start | bytes 804968 | tf_op jit(solution)/shard_map/ppermute | solution.py:19
  90.4 13.8 %copy-start.12 = (bf16[4,128,256]{2,1,0:T(8,128)(2,1)S(1)}, bf16[4,128,256]{2,1,0:T(8,128)(2,1)}, u32[]{:S(2)}) copy-start(bf16[4,128,256]{2,1,0:T(8,128)(2,1)} %param.17) | copy-start | bytes 786436
  101.4 9.7 %collective-permute-start.10 = (f32[1,130,258]{2,1,0:T(8,128)S(1)}, f32[1,130,258]{2,1,0:T(8,128)S(1)}, u32[]{:S(2)}, u32[]{:S(2)}) collective-permute-start(f32[1,130,258]{2,1,0:T(8,128)S(1)} %get-tuple-element.41), channel_id=1, source_target_pairs={{1,0},{3,2},{5,4},{7,6},{9,8},{11,10},{13,12},{15,14},{17,16},{19,... | collective-permute-start | bytes 402488 | tf_op jit(solution)/shard_map/ppermute | solution.py:19
  102.7 8.4 %collective-permute-start.11 = (f32[1,130,258]{2,1,0:T(8,128)S(1)}, f32[1,130,258]{2,1,0:T(8,128)S(1)}, u32[]{:S(2)}, u32[]{:S(2)}) collective-permute-start(f32[1,130,258]{2,1,0:T(8,128)S(1)} %get-tuple-element.42), channel_id=1, source_target_pairs={{0,1},{2,3},{4,5},{6,7},{8,9},{10,11},{12,13},{14,15},{16,17},{18,... | collective-permute-start | bytes 402488 | tf_op jit(solution)/shard_map/ppermute | solution.py:18
  109.9 65.5 %copy-start.6 = (f32[6,130,258]{2,1,0:T(8,128)}, f32[6,130,258]{2,1,0:T(8,128)S(1)}, u32[]{:S(2)}) copy-start(f32[6,130,258]{2,1,0:T(8,128)S(1)} %get-tuple-element.25) | copy-start | bytes 2414884
  111.1 1.0 copy-start.13
  112.1 6.3 %copy-start.24 = (s32[3000]{0:T(1024)S(1)}, s32[3000]{0:T(1024)}, u32[]{:S(2)}) copy-start(s32[3000]{0:T(1024)} %param.24) | copy-start | bytes 36004
  112.1 6.3 %copy-start.25 = (f32[4]{0:T(128)S(1)}, f32[4]{0:T(128)}, u32[]{:S(2)}) copy-start(f32[4]{0:T(128)} %param.27) | copy-start | bytes 52
  112.9 116.5 %copy-start.1 = (f32[4,128,256]{2,1,0:T(8,128)}, f32[4,128,256]{2,1,0:T(8,128)S(1)}, u32[]{:S(2)}) copy-start(f32[4,128,256]{2,1,0:T(8,128)S(1)} %get-tuple-element.18) | copy-start | bytes 1572868
  113.0 8.5 %collective-permute-start.13 = (f32[4,128,1]{2,1,0:T(8,128)S(1)}, f32[4,128,1]{2,1,0:T(8,128)S(1)}, u32[]{:S(2)}, u32[]{:S(2)}) collective-permute-start(f32[4,128,1]{2,1,0:T(8,128)S(1)} %get-tuple-element.61), channel_id=1, source_target_pairs={{0,32},{32,64},{64,96},{1,33},{33,65},{65,97},{2,34},{34,66},{66,9... | collective-permute-start | bytes 6152 | tf_op jit(solution)/shard_map/ppermute | solution.py:18
  117.1 8.3 %collective-permute-start.12 = (f32[4,128,1]{2,1,0:T(8,128)S(1)}, f32[4,128,1]{2,1,0:T(8,128)S(1)}, u32[]{:S(2)}, u32[]{:S(2)}) collective-permute-start(f32[4,128,1]{2,1,0:T(8,128)S(1)} %get-tuple-element.62), channel_id=1, source_target_pairs={{32,0},{64,32},{96,64},{33,1},{65,33},{97,65},{34,2},{66,34},{98,6... | collective-permute-start | bytes 6152 | tf_op jit(solution)/shard_map/ppermute | solution.py:19
  125.5 5.6 %collective-permute-start.15 = (f32[4,1,258]{2,1,0:T(1,128)S(1)}, f32[4,1,258]{2,1,0:T(1,128)S(1)}, u32[]{:S(2)}, u32[]{:S(2)}) collective-permute-start(f32[4,1,258]{2,1,0:T(1,128)S(1)} %get-tuple-element.49), channel_id=1, source_target_pairs={{0,2},{2,4},{4,6},{6,8},{8,10},{10,12},{12,14},{14,16},{16,18},{18... | collective-permute-start | bytes 12392 | tf_op jit(solution)/shard_map/ppermute | solution.py:18
  129.5 4.5 collective-permute-start.14
  134.3 7.1 %collective-permute-start.16 = (f32[1,130,258]{2,1,0:T(8,128)S(1)}, f32[1,130,258]{2,1,0:T(8,128)S(1)}, u32[]{:S(2)}, u32[]{:S(2)}) collective-permute-start(f32[1,130,258]{2,1,0:T(8,128)S(1)} %get-tuple-element.39), channel_id=1, source_target_pairs={{1,0},{3,2},{5,4},{7,6},{9,8},{11,10},{13,12},{15,14},{17,16},{19,... | collective-permute-start | bytes 402488 | tf_op jit(solution)/shard_map/ppermute | solution.py:19
  139.8 3.4 collective-permute-start.17
  144.1 9.1 %collective-permute-start.19 = (f32[4,128,1]{2,1,0:T(8,128)S(1)}, f32[4,128,1]{2,1,0:T(8,128)S(1)}, u32[]{:S(2)}, u32[]{:S(2)}) collective-permute-start(f32[4,128,1]{2,1,0:T(8,128)S(1)} %get-tuple-element.59), channel_id=1, source_target_pairs={{0,32},{32,64},{64,96},{1,33},{33,65},{65,97},{2,34},{34,66},{66,9... | collective-permute-start | bytes 6152 | tf_op jit(solution)/shard_map/ppermute | solution.py:18
  147.7 9.3 %collective-permute-start.18 = (f32[4,128,1]{2,1,0:T(8,128)S(1)}, f32[4,128,1]{2,1,0:T(8,128)S(1)}, u32[]{:S(2)}, u32[]{:S(2)}) collective-permute-start(f32[4,128,1]{2,1,0:T(8,128)S(1)} %get-tuple-element.60), channel_id=1, source_target_pairs={{32,0},{64,32},{96,64},{33,1},{65,33},{97,65},{34,2},{66,34},{98,6... | collective-permute-start | bytes 6152 | tf_op jit(solution)/shard_map/ppermute | solution.py:19
  157.1 5.2 collective-permute-start.21
  160.7 6.5 %collective-permute-start.20 = (f32[4,1,258]{2,1,0:T(1,128)S(1)}, f32[4,1,258]{2,1,0:T(1,128)S(1)}, u32[]{:S(2)}, u32[]{:S(2)}) collective-permute-start(f32[4,1,258]{2,1,0:T(1,128)S(1)} %get-tuple-element.48), channel_id=1, source_target_pairs={{2,0},{4,2},{6,4},{8,6},{10,8},{12,10},{14,12},{16,14},{18,16},{20... | collective-permute-start | bytes 12392 | tf_op jit(solution)/shard_map/ppermute | solution.py:19
  167.4 6.1 %collective-permute-start.22 = (f32[1,130,258]{2,1,0:T(8,128)S(1)}, f32[1,130,258]{2,1,0:T(8,128)S(1)}, u32[]{:S(2)}, u32[]{:S(2)}) collective-permute-start(f32[1,130,258]{2,1,0:T(8,128)S(1)} %get-tuple-element.37), channel_id=1, source_target_pairs={{1,0},{3,2},{5,4},{7,6},{9,8},{11,10},{13,12},{15,14},{17,16},{19,... | collective-permute-start | bytes 402488 | tf_op jit(solution)/shard_map/ppermute | solution.py:19
  171.7 3.4 collective-permute-start.23
  173.5 1.9 copy-start.17
  230.6 8.6 %collective-permute-start.25 = (f32[4,128,1]{2,1,0:T(8,128)S(1)}, f32[4,128,1]{2,1,0:T(8,128)S(1)}, u32[]{:S(2)}, u32[]{:S(2)}) collective-permute-start(f32[4,128,1]{2,1,0:T(8,128)S(1)} %get-tuple-element.57), channel_id=1, source_target_pairs={{0,32},{32,64},{64,96},{1,33},{33,65},{65,97},{2,34},{34,66},{66,9... | collective-permute-start | bytes 6152 | tf_op jit(solution)/shard_map/ppermute | solution.py:18
  233.8 9.2 %collective-permute-start.24 = (f32[4,128,1]{2,1,0:T(8,128)S(1)}, f32[4,128,1]{2,1,0:T(8,128)S(1)}, u32[]{:S(2)}, u32[]{:S(2)}) collective-permute-start(f32[4,128,1]{2,1,0:T(8,128)S(1)} %get-tuple-element.58), channel_id=1, source_target_pairs={{32,0},{64,32},{96,64},{33,1},{65,33},{97,65},{34,2},{66,34},{98,6... | collective-permute-start | bytes 6152 | tf_op jit(solution)/shard_map/ppermute | solution.py:19
  243.1 7.3 %collective-permute-start.27 = (f32[4,1,258]{2,1,0:T(1,128)S(1)}, f32[4,1,258]{2,1,0:T(1,128)S(1)}, u32[]{:S(2)}, u32[]{:S(2)}) collective-permute-start(f32[4,1,258]{2,1,0:T(1,128)S(1)} %get-tuple-element.45), channel_id=1, source_target_pairs={{0,2},{2,4},{4,6},{6,8},{8,10},{10,12},{12,14},{14,16},{16,18},{18... | collective-permute-start | bytes 12392 | tf_op jit(solution)/shard_map/ppermute | solution.py:18
  248.9 4.7 collective-permute-start.26
  253.8 6.0 %collective-permute-start.28 = (f32[1,130,258]{2,1,0:T(8,128)S(1)}, f32[1,130,258]{2,1,0:T(8,128)S(1)}, u32[]{:S(2)}, u32[]{:S(2)}) collective-permute-start(f32[1,130,258]{2,1,0:T(8,128)S(1)} %get-tuple-element.35), channel_id=1, source_target_pairs={{1,0},{3,2},{5,4},{7,6},{9,8},{11,10},{13,12},{15,14},{17,16},{19,... | collective-permute-start | bytes 402488 | tf_op jit(solution)/shard_map/ppermute | solution.py:19
  258.2 3.4 collective-permute-start.29
  259.8 2.1 copy-start.2
  259.8 2.1 copy-start.9
  265.3 29.5 %collective-permute-start.31 = (f32[4,128,1]{2,1,0:T(8,128)}, f32[4,128,1]{2,1,0:T(8,128)S(1)}, u32[]{:S(2)}, u32[]{:S(2)}) collective-permute-start(f32[4,128,1]{2,1,0:T(8,128)} %get-tuple-element.55), channel_id=1, source_target_pairs={{0,32},{32,64},{64,96},{1,33},{33,65},{65,97},{2,34},{34,66},{66,9... | collective-permute-start | bytes 6152 | tf_op jit(solution)/shard_map/ppermute | solution.py:18
  267.2 27.6 %collective-permute-start.30 = (f32[4,128,1]{2,1,0:T(8,128)}, f32[4,128,1]{2,1,0:T(8,128)}, u32[]{:S(2)}, u32[]{:S(2)}) collective-permute-start(f32[4,128,1]{2,1,0:T(8,128)} %get-tuple-element.56), channel_id=1, source_target_pairs={{32,0},{64,32},{96,64},{33,1},{65,33},{97,65},{34,2},{66,34},{98,6... | collective-permute-start | bytes 6152 | tf_op jit(solution)/shard_map/ppermute | solution.py:19
  295.7 6.3 %collective-permute-start.33 = (f32[4,1,258]{2,1,0:T(1,128)S(1)}, f32[4,1,258]{2,1,0:T(1,128)S(1)}, u32[]{:S(2)}, u32[]{:S(2)}) collective-permute-start(f32[4,1,258]{2,1,0:T(1,128)S(1)} %get-tuple-element.43), channel_id=1, source_target_pairs={{0,2},{2,4},{4,6},{6,8},{8,10},{10,12},{12,14},{14,16},{16,18},{18... | collective-permute-start | bytes 12392 | tf_op jit(solution)/shard_map/ppermute | solution.py:18
  299.4 4.7 collective-permute-start.32
  305.2 5.1 collective-permute-start.34
  308.7 3.4 collective-permute-start.35
  310.2 2.1 copy-start.3
  310.3 2.1 copy-start.14
  314.1 8.8 %copy-start.15 = (f32[4,128,256]{2,1,0:T(8,128)}, f32[4,128,256]{2,1,0:T(8,128)S(1)}, u32[]{:S(2)}) copy-start(f32[4,128,256]{2,1,0:T(8,128)S(1)} %fusion.47) | copy-start | bytes 1572868
  314.1 25.4 %copy-start.5 = (bf16[3000,4]{1,0:T(8,128)(2,1)S(1)}, bf16[3000,4]{1,0:T(8,128)(2,1)}, u32[]{:S(2)}) copy-start(bf16[3000,4]{1,0:T(8,128)(2,1)} %copy-done.4) | copy-start | bytes 72004
  314.1 25.4 %copy-start.16 = (f32[3000,4]{1,0:T(8,128)S(1)}, f32[3000,4]{1,0:T(8,128)}, u32[]{:S(2)}) copy-start(f32[3000,4]{1,0:T(8,128)} %gather_fusion.1) | copy-start | bytes 144004
  339.5 209.1 %copy-start.23 = (f32[3000]{0:T(1024)S(1)}, f32[3000]{0:T(1024)}, u32[]{:S(2)}) copy-start(f32[3000]{0:T(1024)} %param.26) | copy-start | bytes 36004
